TPU v7x, 32 devices: a whole 2x2x4 slice. The times are simulated.
32 devices in a mesh: groups: 2 (over y), graph: 8 (over z, x), dp: 2 (over core).
Axes of the slice: x: 2, y: 2, z: 4, core: 2. Of those that a mesh axis runs over, the one named last changes fastest.
Arguments:
- embed: bfloat16 [2, 64, 12544], P('dp', ('groups', 'graph')), parts along dimension 1, may hold values from -6 to 6
- cotangent: bfloat16 [2, 64, 12544], P('dp', ('groups', 'graph')), parts along dimension 1, may hold values from -6 to 6
- rotation: bfloat16 [2, 49, 49, 1024], P('dp', None, None, ('groups', 'graph')), parts along dimension 3, as said below
- distance_feat: bfloat16 [2, 1024, 512], P('dp', ('groups', 'graph')), parts along dimension 1, may hold values from 0 to 1
- src_owner: int32 [2, 1024, 1], P('dp', ('groups', 'graph')), parts along dimension 1, may hold values from 0 to 7; in each aligned block of 64 rows (0 to 63, 64 to 127, ..., all dimensions but the last counted through in order) at most 16 rows name the same one
- src_local: int32 [2, 1024], P('dp', ('groups', 'graph')), parts along dimension 1, may hold values from 0 to 3
- tgt_local: int32 [2, 1024], P('dp', ('groups', 'graph')), parts along dimension 1, may hold values from 0 to 3
- live_count: int32 [2, 16], P('dp', ('groups', 'graph')), parts along dimension 1, may hold values from 16 to 64
- w_src: bfloat16 [256, 256], replicated, may hold values from -0.375 to 0.375
- w_tgt: bfloat16 [256, 256], replicated, may hold values from -0.375 to 0.375
- w_radial: bfloat16 [512, 256], replicated, may hold values from -0.25 to 0.25
Outputs:
- grad_embed: bfloat16 [2, 64, 12544], P('dp', ('groups', 'graph')), parts along dimension 1
- grad_w_src: float32 [512, 256], P('groups'), parts along dimension 0
- grad_w_tgt: float32 [512, 256], P('groups'), parts along dimension 0
- grad_w_radial: float32 [1024, 256], P('groups'), parts along dimension 0
There are 2 independent parts, one for each index of `groups`. A program takes and returns all parts, laid end to end along the dimension named above; an argument that names none is the same for every part. Nothing has to cross between parts.
Inputs may be any that keep to these rules, and one draw needn't show every extreme that they name: `src_owner`: among the 64 edge slots of one device, at most 16 have their source on any one device; this most is reached. The live slots of a device's block are its first live_count ones. `rotation`: block diagonal: entries coupling different degrees are zero.
All inputs are finite; a program needn't handle non-finite values.
Results may differ from a plain program's by a relative error of at most 0.0085.
Values may be sent and summed in bfloat16 or wider, within the bound.
A program may use at most 64 MiB of HBM per device.

v0:
```python
import math

import jax
import jax.numpy as jnp
from jax import lax
from jax.sharding import PartitionSpec as P


def shards(
    embed,
    cotangent,
    rotation,
    distance_feat,
    src_owner,
    src_local,
    tgt_local,
    live_count,
    w_src,
    w_tgt,
    w_radial,
):
    peer_count = lax.axis_size("graph")
    atom_count = embed.shape[1]
    row_len = embed.shape[2]
    coeffs = rotation.shape[1]
    edge_count = rotation.shape[3]
    channels = w_src.shape[0]
    slot_count = max(2, 2 * edge_count // peer_count)
    block_size = math.gcd(edge_count, 32)
    owners = src_owner[0, :, 0]
    local_index = src_local[0]
    matches = (owners[:, None] == jnp.arange(peer_count, dtype=jnp.int32)[None, :]).astype(
        jnp.int32
    )
    before = jnp.cumsum(matches, axis=0) - matches
    slot_rank = jnp.sum(before * matches, axis=1)
    position = owners * slot_count + slot_rank
    placed = position[:, None] == jnp.arange(peer_count * slot_count, dtype=jnp.int32)[None, :]
    wanted = jnp.sum(jnp.where(placed, local_index[:, None], 0), axis=0).reshape(
        peer_count, slot_count
    )
    requested = lax.all_to_all(wanted, "graph", split_axis=0, concat_axis=0, tiled=True)
    own_rows = embed[0]
    outgoing = jnp.take(own_rows, requested.reshape(-1), axis=0).reshape(
        peer_count, slot_count, row_len
    )
    arrived = lax.all_to_all(outgoing, "graph", split_axis=0, concat_axis=0, tiled=True).reshape(
        peer_count * slot_count, row_len
    )
    source_rows = jnp.take(arrived, position, axis=0)
    target_ids = tgt_local[0]
    is_live = jnp.arange(edge_count, dtype=jnp.int32) < live_count[0, 0]
    target_rows = jnp.take(own_rows, target_ids, axis=0)
    cot_rows = jnp.where(
        is_live[:, None], jnp.take(cotangent[0], target_ids, axis=0), jnp.zeros((), jnp.bfloat16)
    )
    rot_all = rotation[0]
    dist_all = distance_feat[0]
    contract_rows = (((0,), (0,)), ((), ()))
    contract_cols = (((1,), (1,)), ((), ()))

    def edge_block(block_index, carry):
        sum_src, sum_tgt, sum_rad, outbound, target_sum = carry
        first = block_index * block_size
        rot_blk = lax.dynamic_slice_in_dim(rot_all, first, block_size, 2)
        src_blk = lax.dynamic_slice_in_dim(source_rows, first, block_size, 0).reshape(
            block_size, coeffs, channels
        )
        tgt_blk = lax.dynamic_slice_in_dim(target_rows, first, block_size, 0).reshape(
            block_size, coeffs, channels
        )
        cot_blk = lax.dynamic_slice_in_dim(cot_rows, first, block_size, 0).reshape(
            block_size, coeffs, channels
        )
        dist_blk = lax.dynamic_slice_in_dim(dist_all, first, block_size, 0)
        ids_blk = lax.dynamic_slice_in_dim(target_ids, first, block_size, 0)
        rot_src = jnp.einsum(
            "ije,ejc->eic", rot_blk, src_blk, preferred_element_type=jnp.float32
        ).astype(jnp.bfloat16)
        rot_tgt = jnp.einsum(
            "ije,ejc->eic", rot_blk, tgt_blk, preferred_element_type=jnp.float32
        ).astype(jnp.bfloat16)
        flat_src = rot_src.reshape(-1, channels)
        flat_tgt = rot_tgt.reshape(-1, channels)
        conv_out = jnp.dot(flat_src, w_src, preferred_element_type=jnp.float32) + jnp.dot(
            flat_tgt, w_tgt, preferred_element_type=jnp.float32
        )
        radial_pre = jnp.dot(dist_blk, w_radial, preferred_element_type=jnp.float32)
        sigmoid_val = jax.nn.sigmoid(radial_pre)
        gate = radial_pre * sigmoid_val
        rot_cot = jnp.einsum(
            "ije,ejc->eic", rot_blk, cot_blk, preferred_element_type=jnp.float32
        ).astype(jnp.bfloat16)
        gate_grad = jnp.sum(
            rot_cot.astype(jnp.float32) * conv_out.reshape(block_size, coeffs, channels), axis=1
        )
        conv_grad = (gate[:, None, :] * rot_cot).astype(jnp.bfloat16)
        flat_grad = conv_grad.reshape(-1, channels)
        pre_grad = (
            gate_grad * (sigmoid_val + radial_pre * sigmoid_val * (1.0 - sigmoid_val))
        ).astype(jnp.bfloat16)
        sum_src = sum_src + lax.dot_general(
            flat_src, flat_grad, contract_rows, preferred_element_type=jnp.float32
        )
        sum_tgt = sum_tgt + lax.dot_general(
            flat_tgt, flat_grad, contract_rows, preferred_element_type=jnp.float32
        )
        sum_rad = sum_rad + lax.dot_general(
            dist_blk, pre_grad, contract_rows, preferred_element_type=jnp.float32
        )
        back_src = lax.dot_general(
            flat_grad, w_src, contract_cols, preferred_element_type=jnp.float32
        ).astype(jnp.bfloat16)
        back_tgt = lax.dot_general(
            flat_grad, w_tgt, contract_cols, preferred_element_type=jnp.float32
        ).astype(jnp.bfloat16)
        back_src = back_src.reshape(block_size, coeffs, channels)
        back_tgt = back_tgt.reshape(block_size, coeffs, channels)
        send_src = jnp.einsum(
            "jie,ejc->eic", rot_blk, back_src, preferred_element_type=jnp.float32
        ).astype(jnp.bfloat16)
        keep_tgt = jnp.einsum(
            "jie,ejc->eic", rot_blk, back_tgt, preferred_element_type=jnp.float32
        ).astype(jnp.bfloat16)
        outbound = lax.dynamic_update_slice_in_dim(
            outbound, send_src.reshape(block_size, row_len), first, 0
        )
        target_hits = (jnp.arange(atom_count, dtype=jnp.int32)[:, None] == ids_blk[None, :]).astype(
            jnp.bfloat16
        )
        target_sum = target_sum + jnp.dot(
            target_hits, keep_tgt.reshape(block_size, row_len), preferred_element_type=jnp.float32
        )
        return (sum_src, sum_tgt, sum_rad, outbound, target_sum)

    initial = (
        jnp.zeros((channels, channels), jnp.float32),
        jnp.zeros((channels, channels), jnp.float32),
        jnp.zeros((w_radial.shape[0], channels), jnp.float32),
        jnp.zeros((edge_count, row_len), jnp.bfloat16),
        jnp.zeros((atom_count, row_len), jnp.float32),
    )
    block_total = edge_count // block_size
    sum_src, sum_tgt, sum_rad, outbound, target_sum = lax.fori_loop(
        0, block_total, edge_block, initial
    )
    bucket = jnp.zeros((peer_count * slot_count, row_len), jnp.bfloat16).at[position].set(outbound)
    returned = lax.all_to_all(
        bucket.reshape(peer_count, slot_count, row_len),
        "graph",
        split_axis=0,
        concat_axis=0,
        tiled=True,
    )
    returned = returned.reshape(peer_count * slot_count, row_len)
    owner_hits = (
        jnp.arange(atom_count, dtype=jnp.int32)[:, None] == requested.reshape(-1)[None, :]
    ).astype(jnp.bfloat16)
    source_sum = jnp.dot(owner_hits, returned, preferred_element_type=jnp.float32)
    grad_embed = (source_sum + target_sum).astype(jnp.bfloat16)[None]
    total_src, total_tgt, total_rad = lax.psum((sum_src, sum_tgt, sum_rad), ("graph", "dp"))
    scale = 1.0 / math.sqrt(lax.axis_size("dp") * edge_count * peer_count * coeffs)
    return (grad_embed, total_src * scale, total_tgt * scale, total_rad * scale)


def solution(mesh):
    placed = (
        P("dp", ("groups", "graph"), None),
        P("dp", ("groups", "graph"), None),
        P("dp", None, None, ("groups", "graph")),
        P("dp", ("groups", "graph"), None),
        P("dp", ("groups", "graph"), None),
        P("dp", ("groups", "graph")),
        P("dp", ("groups", "graph")),
        P("dp", ("groups", "graph")),
        P(),
        P(),
        P(),
    )
    return jax.shard_map(
        shards,
        mesh=mesh,
        in_specs=placed,
        out_specs=(
            P("dp", ("groups", "graph"), None),
            P("groups", None),
            P("groups", None),
            P("groups", None),
        ),
        check_vma=False,
    )
```

profile of v0, /device:TPU:0, one launch (start us, length us, event | category | flops | bytes accessed | tf_op | source)
XLA Modules:
  0.0 361.4 jit_solution(7602301279370179071)
XLA Ops:
  10.4 13.5 %all_to_all.19 = s32[8,1,16]{2,1,0:T(1,128)S(1)} all-to-all(s32[8,1,16]{2,1,0:T(1,128)S(1)} %bitcast.129), channel_id=1, replica_groups=mesh['groups'=2,'graph'=8,'dp'=2] {'graph'}, dimensions={0} | all-to-all | bytes 1024 | tf_op jit(solution)/shard_map/all_to_all | solution.py:42
  24.0 2.6 gather_fusion
  26.6 2.1 broadcast_select_fusion
  28.7 3.8 %all-to-all-start.1 = ((bf16[8,16,12544]{2,1,0:T(8,128)(2,1)}), bf16[8,16,12544]{2,1,0:T(8,128)(2,1)S(1)}, u32[]{:S(2)}, u32[]{:S(2)}) async-start(bf16[8,16,12544]{2,1,0:T(8,128)(2,1)} %broadcast_select_fusion), calls=%async_computation.1 | async-start | bytes 6422528 | tf_op jit(solution)/shard_map/all_to_all | solution.py:47
  32.6 2.8 gather_fusion.3
  35.3 2.7 gather_fusion.2
  38.7 3.4 copy.28
  42.2 3.9 %broadcast_select_fusion.1 = (bf16[64,12544]{1,0:T(8,128)(2,1)}, bf16[64,12544]{1,0:T(8,128)(2,1)}) fusion(bf16[64,12544]{1,0:T(8,128)(2,1)} %gather_fusion.3, pred[64]{0:T(512)(128)(4,1)S(1)} %get-tuple-element.349, bf16[64,12544]{1,0:T(8,128)(2,1)} %gather_fusion.2, pred[64]{0:T(512)(128)(4,1)S(1)} %get-tuple-element.350), kind=kLoop, calls=%fused_computation.56 | loop fusion | flops 2408448 | bytes 6422656 | tf_op jit(solution)/shard_map/jit(_take)/select_n | solution.py:53
  46.1 57.2 %all-to-all-done.1 = bf16[8,16,12544]{2,1,0:T(8,128)(2,1)S(1)} async-done(((bf16[8,16,12544]{2,1,0:T(8,128)(2,1)}), bf16[8,16,12544]{2,1,0:T(8,128)(2,1)S(1)}, u32[]{:S(2)}, u32[]{:S(2)}) %all-to-all-start.1) | async-done | bytes 3211296 | tf_op jit(solution)/shard_map/all_to_all | solution.py:47
  103.4 2.8 gather_fusion.1
  106.1 2.8 broadcast_select_fusion.2
  110.2 85.1 %while.22 = (s32[]{:T(128)}, f32[256,256]{1,0:T(8,128)}, f32[256,256]{1,0:T(8,128)}, f32[512,256]{1,0:T(8,128)}, bf16[64,12544]{1,0:T(8,128)(2,1)}, /*index=5*/f...) while((s32[]{:T(128)}, f32[256,256]{1,0:T(8,128)}, ...), condition=%wide.region_5.7_spmd.clone, body=%wide.region_3.6_spmd.clone.sunk | while | flops 1455745152 | bytes 90235952 | solution.py:144
  114.9 2.2 constant_dynamic-slice_fusion.6
  121.5 2.7 convolution_add_fusion.7
  124.1 2.8 reshape.289
  129.0 2.5 fusion.108
  132.7 2.4 convolution_convert_fusion.15
  135.2 2.3 reshape.292
  142.2 2.3 reshape.293
  147.4 2.1 convolution_add_fusion.9
  157.0 2.2 constant_dynamic-slice_fusion.6
  163.5 2.7 convolution_add_fusion.7
  166.2 2.8 reshape.289
  171.1 2.5 fusion.108
  174.8 2.4 convolution_convert_fusion.15
  177.2 2.3 reshape.292
  184.2 2.3 reshape.293
  189.5 2.1 convolution_add_fusion.9
  193.2 2.1 fusion.109
  195.3 5.7 %scatter_custom_fusion = bf16[128,12544]{1,0:T(8,128)(2,1)} fusion(s32[64]{0:T(128)S(1)} %fusion.30, bf16[64,12544]{1,0:T(8,128)(2,1)} %get-tuple-element.253, bf16[]{:T(256)} %constant.92.clone.1), kind=kCustom, calls=%fused_computation.54 | custom fusion | bytes 3211776 | tf_op jit(solution)/shard_map/scatter | solution.py:147
  201.0 3.7 %all-to-all-start.2 = ((bf16[8,16,12544]{2,1,0:T(8,128)(2,1)}), bf16[8,16,12544]{2,1,0:T(8,128)(2,1)S(1)}, u32[]{:S(2)}, u32[]{:S(2)}) async-start(bf16[8,16,12544]{2,1,0:T(8,128)(2,1)} %bitcast.124), calls=%async_computation.2 | async-start | bytes 6422528 | tf_op jit(solution)/shard_map/all_to_all | solution.py:148
  206.6 141.6 %all-reduce.3.cloned.1.call-done = (f32[256,256]{1,0:T(8,128)}, f32[256,256]{1,0:T(8,128)}, f32[512,256]{1,0:T(8,128)}) async-done(((f32[256,256]{1,0:T(8,128)}, f32[256,256]{1,0:T(8,128)}, f32[512,256]{1,0:T(8,128)}), (f32[256,256]{1,0:T(8,128)}, f32[256,256]{1,0:T(8,128)}, f32[512,256]{1,0:T(8,128)})) %all-reduce.3.cloned.1.call-update) | async-done | bytes 1048592 | tf_op jit(solution)/shard_map/psum | solution.py:161
  (141 shorter events, 57.2 us)
Async XLA Ops:
  7.2 16.8 %copy-start = (bf16[1,4,12544]{2,1,0:T(4,128)(2,1)S(1)}, bf16[1,4,12544]{2,1,0:T(4,128)(2,1)}, u32[]{:S(2)}) copy-start(bf16[1,4,12544]{2,1,0:T(4,128)(2,1)} %param.15) | copy-start | bytes 301060
  28.7 3.8 %copy-start.19 = (s32[1,64]{1,0:T(1,128)S(1)}, s32[1,64]{1,0:T(1,128)}, u32[]{:S(2)}) copy-start(s32[1,64]{1,0:T(1,128)} %param.21) | copy-start | bytes 772
  28.7 74.7 %all-to-all-start.1 = ((bf16[8,16,12544]{2,1,0:T(8,128)(2,1)}), bf16[8,16,12544]{2,1,0:T(8,128)(2,1)S(1)}, u32[]{:S(2)}, u32[]{:S(2)}) async-start(bf16[8,16,12544]{2,1,0:T(8,128)(2,1)} %broadcast_select_fusion), calls=%async_computation.1 | async-start | bytes 6422528 | tf_op jit(solution)/shard_map/all_to_all | solution.py:47
  32.5 2.8 copy-start.1
  38.1 4.1 %copy-start.18 = (s32[1,64,1]{1,2,0:T(1,128)S(1)}, s32[1,64,1]{1,2,0:T(1,128)}, u32[]{:S(2)}) copy-start(s32[1,64,1]{1,2,0:T(1,128)} %param.19) | copy-start | bytes 772
  113.5 1.5 copy-start.4
  124.1 2.8 copy-start.12
  124.1 2.8 copy-start.14
  124.1 3.6 copy-start.3
  137.4 2.1 copy-start.16
  139.3 1.4 copy-start.2
  139.3 1.4 copy-start.8
  146.2 3.3 copy-start.5
  146.2 3.3 copy-start.13
  146.2 3.3 copy-start.15
  147.4 2.4 copy-start.9
  149.8 2.4 copy-start.6
  155.5 1.5 copy-start.4
  166.2 2.8 copy-start.12
  166.2 2.8 copy-start.14
  166.2 3.6 copy-start.3
  179.5 2.1 copy-start.16
  181.4 1.4 copy-start.2
  181.4 1.4 copy-start.8
  188.3 3.3 copy-start.5
  188.3 3.3 copy-start.13
  188.3 3.3 copy-start.15
  189.5 2.5 copy-start.9
  191.9 3.3 copy-start.6
  201.0 152.5 %all-to-all-start.2 = ((bf16[8,16,12544]{2,1,0:T(8,128)(2,1)}), bf16[8,16,12544]{2,1,0:T(8,128)(2,1)S(1)}, u32[]{:S(2)}, u32[]{:S(2)}) async-start(bf16[8,16,12544]{2,1,0:T(8,128)(2,1)} %bitcast.124), calls=%async_computation.2 | async-start | bytes 6422528 | tf_op jit(solution)/shard_map/all_to_all | solution.py:148
  204.6 148.8 %copy-start.11 = (f32[4,12544]{1,0:T(4,128)S(1)}, f32[4,12544]{1,0:T(4,128)}, u32[]{:S(2)}) copy-start(f32[4,12544]{1,0:T(4,128)} %get-tuple-element.254) | copy-start | bytes 602116
  204.6 143.5 %all-reduce.3.cloned.1.call-start = ((), (), s32[]{:S(2)}) async-start(), calls=%async_computation.3 | async-start | bytes 2097152 | tf_op jit(solution)/shard_map/psum | solution.py:161
  (6 other events, 6.2 us)
Sparse Core Ops, SparseCore 0:
  209.9 138.2 all-reduce.2
where the time goes:
time: 363 us; the launch traced here: 361 us
  waiting for transfers between devices  199 us (55%)
  local copies, waits for them, and re-layouts  61.8 us (17%)
  matrix products  46.1 us (13%)
  other arithmetic  17.9 us (5%)
  between operations  14.9 us (4%)
  blocking collectives  13.5 us (4%)
  starting transfers between devices  7.48 us (2%)
    psum x1, waiting for transfers between devices, shards(): lax.psum((sum_src, sum_tgt, sum_rad), ('graph', 'dp'))  142 us
    all_to_all x1, waiting for transfers between devices, shards(): lax.all_to_all(outgoing, 'graph', split_axis=0, concat_axis=0, tiled=True)  57.2 us
    all_to_all x1, blocking collectives, shards(): lax.all_to_all(wanted, 'graph', split_axis=0, concat_axis=0, tiled=True)  13.5 us
  transfers between devices with their start and end apart: 3, of which 2 were waited for; matrix products, arithmetic and copies ran while one was open for 5% of the time, Pallas kernels for 0%

commit v1 on v0

--- a/solution.py
+++ b/solution.py
@@ -1,8 +1,11 @@
+import functools
 import math
 
 import jax
 import jax.numpy as jnp
 from jax import lax
+from jax.experimental import pallas as pl
+from jax.experimental.pallas import tpu as pltpu
 from jax.sharding import PartitionSpec as P
 
 
@@ -163,7 +166,395 @@
     return (grad_embed, total_src * scale, total_tgt * scale, total_rad * scale)
 
 
+def remote(src, dst, send_sem, recv_sem, device):
+    return pltpu.make_async_remote_copy(
+        src_ref=src,
+        dst_ref=dst,
+        send_sem=send_sem,
+        recv_sem=recv_sem,
+        device_id=device,
+        device_id_type=pl.DeviceIdType.MESH,
+    )
+
+
+def dot(a, b, dims=(((1,), (0,)), ((), ()))):
+    return lax.dot_general(a, b, dims, preferred_element_type=jnp.float32)
+
+
+FIRST = (((0,), (0,)), ((), ()))
+LAST = (((1,), (1,)), ((), ()))
+
+
+def block_kernel(
+    peers,
+    scale,
+    emb,
+    cot,
+    rot,
+    dist,
+    keys,
+    tgt,
+    live,
+    w_src,
+    w_tgt,
+    w_rad,
+    out_embed,
+    out_src,
+    out_tgt,
+    out_rad,
+    atoms,
+    y_all,
+    y_tgt,
+    rot_rows,
+    cot_rows,
+    cot_half,
+    held,
+    gate,
+    slope,
+    pick,
+    place,
+    sums,
+    kept,
+    from_x,
+    to_z,
+    from_z,
+    part_tgt,
+    part_rad,
+    part_src,
+    core_tgt,
+    core_rad,
+    core_src,
+    early,
+    early_in,
+    late,
+    late_in,
+    whole,
+    y_send,
+    y_recv,
+    f_send,
+    x_send,
+    x_recv,
+    z_send,
+    z_recv,
+    c_send,
+    c_recv,
+    e_send,
+    e_recv,
+    l_send,
+    l_recv,
+    g_send,
+    g_recv,
+    h_send,
+    h_recv,
+):
+    coeffs, edges, width = rot.shape[0], rot.shape[2], w_src.shape[0]
+    atom_count = emb.shape[0]
+    groups = -(-coeffs // 4)
+    tall = rot_rows.shape[0] // edges
+    deep = cot_half.shape[1]
+    columns = peers // 2
+    parts = width // 128
+    me, core = lax.axis_index("graph"), lax.axis_index("dp")
+    z, x = lax.div(me, 2), lax.rem(me, 2)
+    beside = {"graph": z * 2 + 1 - x}
+    other = {"dp": 1 - core}
+    started = []
+
+    def send(*args):
+        copy = remote(*args)
+        copy.start()
+        started.append(copy)
+
+    def wide(ref, first, last):
+        return jnp.concatenate([ref[part, first:last, :] for part in range(parts)], axis=1)
+
+    def arrived(ref, sem):
+        remote(ref, ref, sem, sem, other).wait_recv()
+
+    barrier = pltpu.get_barrier_semaphore()
+    for step in range(1, peers):
+        pl.semaphore_signal(
+            barrier,
+            inc=1,
+            device_id={"graph": lax.rem(me + step, peers)},
+            device_id_type=pl.DeviceIdType.MESH,
+        )
+    pl.semaphore_signal(barrier, inc=1, device_id=other, device_id_type=pl.DeviceIdType.MESH)
+
+    for group in range(groups):
+        rows = []
+        for c in range(4 * group, 4 * group + 4):
+            if c < coeffs:
+                rows.append(emb[:, c * width : (c + 1) * width].astype(jnp.float32))
+            else:
+                rows.append(jnp.zeros((atom_count, width), jnp.float32))
+        atoms[16 * group : 16 * group + 16, :] = jnp.concatenate(rows, axis=0).astype(jnp.bfloat16)
+    y_all[me] = dot(atoms[...], w_src[...]).astype(jnp.bfloat16)
+    pl.semaphore_wait(barrier, peers)
+    for step in range(1, columns):
+        to = {"graph": lax.rem(z + step, columns) * 2 + x}
+        send(y_all.at[me], y_all.at[me], y_send.at[step], y_recv.at[me], to)
+    send(y_all.at[me], y_all.at[me], y_send.at[0], y_recv.at[me], beside)
+    y_tgt[...] = dot(atoms[...], w_tgt[...]).astype(jnp.bfloat16)
+
+    pre = dot(dist[...], w_rad[...])
+    sig = jax.nn.sigmoid(pre)
+    alive = lax.broadcasted_iota(jnp.int32, (edges, width), 0) < live[0, 0]
+    gate[...] = jnp.where(alive, pre * sig, 0.0)
+    slope[...] = jnp.where(alive, sig + pre * sig * (1.0 - sig), 0.0)
+
+    row = lax.broadcasted_iota(jnp.int32, (256, 256), 0)
+    k, a = lax.rem(lax.div(row, 4), 4), lax.rem(row, 4)
+    src_rows = 16 * peers
+    key_src = jnp.broadcast_to(keys[0:1, :], (256, 256))
+    key_tgt = jnp.broadcast_to(keys[1:2, :], (256, 256))
+    hit_src = (k * (4 * peers) + lax.div(row, 16) * 4 + a) == key_src
+    hit_tgt = (k * 4 + a) == key_tgt
+    hit = ((row < src_rows) & hit_src) | ((row >= src_rows) & (row < src_rows + 16) & hit_tgt)
+    ones = jnp.where(hit, 1.0, 0.0)
+    pick[...] = ones.astype(jnp.bfloat16)
+    place[...] = ones.T.astype(jnp.bfloat16)
+
+    rot_rows[...] = jnp.zeros_like(rot_rows)
+    cot_rows[...] = jnp.zeros_like(cot_rows)
+    for c in range(coeffs):
+        block = rot[c].astype(jnp.float32)
+        block = jnp.concatenate([block, jnp.zeros((deep - coeffs, edges), jnp.float32)], axis=0)
+        rot_rows[c * edges : (c + 1) * edges, 0:deep] = block.T
+        line = cot[:, c * width : (c + 1) * width].astype(jnp.float32)
+        for part in range(parts):
+            cot_rows[part, pl.ds(c, atom_count, stride=deep), :] = line[:, part * 128 : part * 128 + 128]
+    cot_half[...] = wide(cot_rows, 0, atom_count * deep).reshape(cot_half.shape).astype(jnp.bfloat16)
+
+    def edge(e, unused):
+        r = rot_rows[pl.ds(e, tall, stride=edges), :][:, 0:deep].astype(jnp.bfloat16)
+        turned = dot(r, cot_half[tgt[0, e]]).astype(jnp.bfloat16)
+        back = dot(r, turned, FIRST)[0:tall]
+        for part in range(parts):
+            held[part, pl.ds(e, tall, stride=edges), :] = back[:, part * 128 : part * 128 + 128]
+        return unused
+
+    def forward(step):
+        block = lax.rem(z - step + columns, columns) * 2 + x
+        arrived(y_all.at[block], y_recv.at[block])
+        send(y_all.at[block], y_all.at[block], f_send.at[step], y_recv.at[block], beside)
+
+    for part in range(4):
+        lax.fori_loop(part * (edges // 4), (part + 1) * (edges // 4), edge, 0, unroll=8)
+        if 1 <= part < columns:
+            forward(part)
+    for step in range(4, columns):
+        forward(step)
+
+    for group in range(groups):
+        rows = slice(group * 4 * edges, (group + 1) * 4 * edges)
+        gated = wide(held, rows.start, rows.stop).reshape(4, edges, width) * gate[...][None]
+        total = dot(pick[...], gated.reshape(4 * edges, width).astype(jnp.bfloat16))
+        for p in range(peers):
+            sums[p, 16 * group : 16 * group + 16, :] = total[16 * p : 16 * p + 16].astype(
+                jnp.bfloat16
+            )
+        kept[16 * group : 16 * group + 16, :] = total[src_rows : src_rows + 16].astype(jnp.bfloat16)
+    for step in list(range(1, columns)) + [0]:
+        goal = lax.rem(z + step, columns)
+        send(sums.at[goal * 2 + 1 - x], from_x.at[goal], x_send.at[step], x_recv.at[goal], beside)
+
+    half = width // 2
+    part_tgt[...] = (
+        dot(atoms[...], kept[...], FIRST).astype(jnp.bfloat16).reshape(part_tgt.shape)
+    )
+    send(part_tgt.at[1 - core], core_tgt, c_send.at[0], c_recv.at[0], other)
+
+    for step in range(columns):
+        block = step * 2 + 1 - x
+        arrived(y_all.at[block], y_recv.at[block])
+    gate_grad = jnp.zeros((edges, width), jnp.float32)
+    spare = jnp.zeros((256 - src_rows - 16, width), jnp.bfloat16)
+    for group in range(groups):
+        near = [y_all[p, 16 * group : 16 * group + 16, :] for p in range(peers)]
+        near = jnp.concatenate(near + [y_tgt[16 * group : 16 * group + 16, :], spare], axis=0)
+        mixed = dot(place[...], near) * wide(
+            held, group * 4 * edges, (group + 1) * 4 * edges
+        )
+        gate_grad = gate_grad + jnp.sum(mixed.reshape(4, edges, width), axis=0)
+    pre_grad = (gate_grad * slope[...]).astype(jnp.bfloat16)
+    part_rad[...] = dot(dist[...], pre_grad, FIRST).astype(jnp.bfloat16).reshape(part_rad.shape)
+    send(part_rad.at[1 - core], core_rad, c_send.at[1], c_recv.at[1], other)
+
+    for step in range(1, columns):
+        goal = lax.rem(z + step, columns)
+        arrived(from_x.at[goal], x_recv.at[goal])
+        to_z[goal] = (
+            sums[goal * 2 + x].astype(jnp.float32) + from_x[goal].astype(jnp.float32)
+        ).astype(jnp.bfloat16)
+        send(to_z.at[goal], from_z.at[z], z_send.at[step], z_recv.at[z], {"graph": goal * 2 + x})
+
+    arrived(core_tgt, c_recv.at[0])
+    arrived(core_rad, c_recv.at[1])
+    cut_tgt, cut_rad = half // peers, w_rad.shape[0] // 2 // peers
+    both_tgt = part_tgt[core].astype(jnp.float32) + core_tgt[...].astype(jnp.float32)
+    both_rad = part_rad[core].astype(jnp.float32) + core_rad[...].astype(jnp.float32)
+    early[:, 0:cut_tgt, :] = both_tgt.reshape(peers, cut_tgt, width).astype(jnp.bfloat16)
+    early[:, cut_tgt:, :] = both_rad.reshape(peers, cut_rad, width).astype(jnp.bfloat16)
+    for step in range(1, peers):
+        p = lax.rem(me + step, peers)
+        send(early.at[p], early_in.at[me], e_send.at[step], e_recv.at[me], {"graph": p})
+
+    arrived(from_x.at[z], x_recv.at[z])
+    total = sums[me].astype(jnp.float32) + from_x[z].astype(jnp.float32)
+    for step in range(1, columns):
+        origin = lax.rem(z + step, columns)
+        arrived(from_z.at[origin], z_recv.at[origin])
+        total = total + from_z[origin].astype(jnp.float32)
+    total = total.astype(jnp.bfloat16)
+    part_src[...] = dot(atoms[...], total, FIRST).astype(jnp.bfloat16).reshape(part_src.shape)
+    send(part_src.at[1 - core], core_src, c_send.at[2], c_recv.at[2], other)
+    back = dot(total, w_src[...], LAST) + dot(kept[...], w_tgt[...], LAST)
+    for c in range(coeffs):
+        out_embed[:, c * width : (c + 1) * width] = back[4 * c : 4 * c + 4].astype(jnp.bfloat16)
+    arrived(core_src, c_recv.at[2])
+    both_src = part_src[core].astype(jnp.float32) + core_src[...].astype(jnp.float32)
+    late[...] = both_src.reshape(late.shape).astype(jnp.bfloat16)
+    for step in range(1, peers):
+        p = lax.rem(me + step, peers)
+        send(late.at[p], late_in.at[me], l_send.at[step], l_recv.at[me], {"graph": p})
+
+    first = early[me].astype(jnp.float32)
+    second = late[me].astype(jnp.float32)
+    for step in range(1, peers):
+        p = lax.rem(me + step, peers)
+        arrived(early_in.at[p], e_recv.at[p])
+        first = first + early_in[p].astype(jnp.float32)
+    for step in range(1, peers):
+        p = lax.rem(me + step, peers)
+        arrived(late_in.at[p], l_recv.at[p])
+        second = second + late_in[p].astype(jnp.float32)
+    split = cut_tgt + cut_rad
+    whole[core, me, 0:split, :] = first.astype(jnp.bfloat16)
+    whole[core, me, split:, :] = second.astype(jnp.bfloat16)
+    mine = whole.at[core, me]
+    for step in range(1, peers):
+        p = lax.rem(me + step, peers)
+        send(mine, mine, g_send.at[step], g_recv.at[me], {"graph": p})
+    send(mine, mine, h_send.at[0], h_recv.at[me], other)
+
+    def spread(c, p):
+        piece = whole[c, p].astype(jnp.float32) * scale
+        at_tgt = pl.ds(pl.multiple_of(c * half + p * cut_tgt, cut_tgt), cut_tgt)
+        at_rad = pl.ds(pl.multiple_of((c * peers + p) * cut_rad, cut_rad), cut_rad)
+        out_tgt[at_tgt, :] = piece[0:cut_tgt]
+        out_rad[at_rad, :] = piece[cut_tgt:split]
+        out_src[at_tgt, :] = piece[split:]
+
+    spread(core, me)
+    for step in range(1, peers):
+        p = lax.rem(me + step, peers)
+        arrived(whole.at[core, p], g_recv.at[p])
+        send(whole.at[core, p], whole.at[core, p], h_send.at[step], h_recv.at[p], other)
+        spread(core, p)
+    for step in range(peers):
+        p = lax.rem(me + step, peers)
+        arrived(whole.at[1 - core, p], h_recv.at[p])
+        spread(1 - core, p)
+    for copy in started:
+        copy.wait_send()
+
+
+def near_shards(
+    embed,
+    cotangent,
+    rotation,
+    distance_feat,
+    src_owner,
+    src_local,
+    tgt_local,
+    live_count,
+    w_src,
+    w_tgt,
+    w_radial,
+):
+    peers = lax.axis_size("graph")
+    columns = peers // 2
+    atom_count, row_len = embed.shape[1:]
+    coeffs, edges = rotation.shape[1], rotation.shape[3]
+    width, radial = w_src.shape[0], w_radial.shape[0]
+    groups = -(-coeffs // 4)
+    tall = -(-groups * 4 // 8) * 8
+    deep = -(-tall // 16) * 16
+    scale = 1.0 / math.sqrt(lax.axis_size("dp") * edges * peers * coeffs)
+    lane = jnp.arange(4, dtype=jnp.int32)[:, None]
+    key_src = lane * (4 * peers) + (src_owner[0, :, 0] * atom_count + src_local[0])[None, :]
+    key_tgt = lane * 4 + tgt_local[0][None, :]
+    keys = jnp.stack([key_src.reshape(-1), key_tgt.reshape(-1)])
+    half, cut = width // 2, width // 2 // peers
+    rows = 16 * groups
+    bf16, f32 = jnp.bfloat16, jnp.float32
+    split = cut + radial // 2 // peers
+    vmem = pl.BlockSpec(memory_space=pltpu.VMEM)
+    smem = pl.BlockSpec(memory_space=pltpu.SMEM)
+    dma = pltpu.SemaphoreType.DMA
+    scratch = [
+        pltpu.VMEM((rows, width), bf16),
+        pltpu.VMEM((peers, rows, width), bf16),
+        pltpu.VMEM((rows, width), bf16),
+        pltpu.VMEM((tall * edges, 128), f32),
+        pltpu.VMEM((width // 128, atom_count * deep, 128), f32),
+        pltpu.VMEM((atom_count, deep, width), bf16),
+        pltpu.VMEM((width // 128, tall * edges, 128), f32),
+        pltpu.VMEM((edges, width), f32),
+        pltpu.VMEM((edges, width), f32),
+        pltpu.VMEM((256, 256), bf16),
+        pltpu.VMEM((256, 256), bf16),
+        pltpu.VMEM((peers, rows, width), bf16),
+        pltpu.VMEM((rows, width), bf16),
+        pltpu.VMEM((columns, rows, width), bf16),
+        pltpu.VMEM((columns, rows, width), bf16),
+        pltpu.VMEM((columns, rows, width), bf16),
+        pltpu.VMEM((2, half, width), bf16),
+        pltpu.VMEM((2, radial // 2, width), bf16),
+        pltpu.VMEM((2, half, width), bf16),
+        pltpu.VMEM((half, width), bf16),
+        pltpu.VMEM((radial // 2, width), bf16),
+        pltpu.VMEM((half, width), bf16),
+        pltpu.VMEM((peers, split, width), bf16),
+        pltpu.VMEM((peers, split, width), bf16),
+        pltpu.VMEM((peers, cut, width), bf16),
+        pltpu.VMEM((peers, cut, width), bf16),
+        pltpu.VMEM((2, peers, split + cut, width), bf16),
+    ]
+    counts = [peers, peers, columns, columns, columns, columns, columns, 3, 3] + [peers] * 8
+    grad_embed, grad_src, grad_tgt, grad_rad = pl.pallas_call(
+        functools.partial(block_kernel, peers, scale),
+        out_shape=(
+            jax.ShapeDtypeStruct((atom_count, row_len), bf16),
+            jax.ShapeDtypeStruct((width, width), f32),
+            jax.ShapeDtypeStruct((width, width), f32),
+            jax.ShapeDtypeStruct((radial, width), f32),
+        ),
+        in_specs=[vmem] * 5 + [smem] * 2 + [vmem] * 3,
+        out_specs=(vmem,) * 4,
+        scratch_shapes=scratch + [dma((count,)) for count in counts],
+        compiler_params=pltpu.CompilerParams(
+            collective_id=0, has_side_effects=True, vmem_limit_bytes=40 * 1024 * 1024
+        ),
+    )(
+        embed[0],
+        cotangent[0],
+        rotation[0],
+        distance_feat[0],
+        keys,
+        tgt_local,
+        live_count,
+        w_src,
+        w_tgt,
+        w_radial,
+    )
+    return grad_embed[None], grad_src, grad_tgt, grad_rad
+
+
 def solution(mesh):
+    peers = mesh.shape["graph"]
+    near = peers in (4, 8) and mesh.shape["dp"] == 2
     placed = (
         P("dp", ("groups", "graph"), None),
         P("dp", ("groups", "graph"), None),
@@ -178,7 +569,7 @@
         P(),
     )
     return jax.shard_map(
-        shards,
+        near_shards if near else shards,
         mesh=mesh,
         in_specs=placed,
         out_specs=(

time: 363 us -> 62.4 us (0.17)
  waiting for transfers between devices: 199 us -> 0 us
  local copies, waits for them, and re-layouts: 61.8 us -> 10.7 us
  Pallas kernels: 0 us -> 49.8 us
  matrix products: 46.1 us -> 0 us
  other arithmetic: 17.9 us -> 0.16 us
  between operations: 14.9 us -> 1.32 us
  blocking collectives: 13.5 us -> 0 us
  starting transfers between devices: 7.48 us -> 0 us
    psum x1 -> x0, waiting for transfers between devices: 142 us -> none  [shards(): lax.psum((sum_src, sum_tgt, sum_rad), ('graph', 'dp'))]
    all_to_all x2 -> x0, waiting for transfers between devices: 57.2 us -> none  [the longest x1 57.2 us: shards(): lax.all_to_all(outgoing, 'graph', split_axis=0, concat_axis=0, tiled=True)]
    pallas_call x0 -> x1, Pallas kernels: none -> 49.8 us  [near_shards(): pl.pallas_call(functools.partial(block_kernel, peers, scale), out_shape=(...]
    dot_general x29 -> x0, matrix products: 46.1 us -> none  [the longest x2 5.35 us: edge_block(): jnp.dot(flat_tgt, w_tgt, preferred_element_type=jnp.float32)]
    reshape x19 -> x0, local copies, waits for them, and re-layouts: 26.4 us -> none  [the longest x2 5.66 us: edge_block(): conv_out.reshape(block_size, coeffs, channels)]
    all_to_all x1 -> x0, blocking collectives: 13.5 us -> none  [shards(): lax.all_to_all(wanted, 'graph', split_axis=0, concat_axis=0, tiled=True)]
    gather x4 -> x0, local copies, waits for them, and re-layouts: 10.8 us -> none  [the longest x1 2.77 us: shards(): target_rows = jnp.take(own_rows, target_ids, axis=0)]
    select_n x6 -> x0, other arithmetic: 8.83 us -> none  [the longest x1 3.94 us: shards(): target_rows = jnp.take(own_rows, target_ids, axis=0)]
  transfers between devices with their start and end apart: 3 -> 0, of which waited for: 2 -> 0; matrix products, arithmetic and copies ran while one was open for 5% -> 0% of each run, Pallas kernels for 0% -> 0%
where the time goes in v1:
time: 62.4 us; the launch traced here: 62 us
  Pallas kernels  49.8 us (80%)
  local copies, waits for them, and re-layouts  10.7 us (17%)
  between operations  1.32 us (2%)
    pallas_call x1, Pallas kernels, near_shards(): pl.pallas_call(functools.partial(block_kernel, peers, scale), out_shape=(...  49.8 us
    unnamed x24, local copies, waits for them, and re-layouts  10.6 us

profile of v1, /device:TPU:0, one launch (start us, length us, event | category | flops | bytes accessed | tf_op | source)
XLA Modules:
  0.0 62.0 jit_solution(751877595752979044)
XLA Ops:
  1.3 0.0 copy-start.8
  1.3 0.0 copy-start.9
  1.3 0.6 %copy-done.8 = s32[1,64]{1,0:T(1,128)S(1)} copy-done((s32[1,64]{1,0:T(1,128)S(1)}, s32[1,64]{1,0:T(1,128)}, u32[]{:S(2)}) %copy-start.8) | copy-done | bytes 280
  1.9 0.0 copy-done.9
  2.0 0.1 broadcast_add_fusion.1
  2.0 0.0 copy-start.7
  2.0 0.1 add.59
  2.1 0.6 copy-done.7
  2.7 0.1 broadcast_add_fusion
  2.8 0.1 add.64
  2.9 0.0 copy-start
  2.9 1.1 %copy-done = bf16[1,49,49,64]{3,2,1,0:T(8,128)(2,1)S(1)} copy-done((bf16[1,49,49,64]{3,2,1,0:T(8,128)(2,1)S(1)}, bf16[1,49,49,64]{3,2,1,0:T(8,128)(2,1)}, u32[]{:S(2)}) %copy-start) | copy-done | bytes 307352
  4.0 0.0 copy-start.1
  4.0 0.9 %copy-done.1 = bf16[512,256]{1,0:T(8,128)(2,1)S(1)} copy-done((bf16[512,256]{1,0:T(8,128)(2,1)S(1)}, bf16[512,256]{1,0:T(8,128)(2,1)}, u32[]{:S(2)}) %copy-start.1) | copy-done | bytes 262168
  4.9 0.0 copy-start.2
  4.9 0.9 %copy-done.2 = bf16[256,256]{1,0:T(8,128)(2,1)S(1)} copy-done((bf16[256,256]{1,0:T(8,128)(2,1)S(1)}, bf16[256,256]{1,0:T(8,128)(2,1)}, u32[]{:S(2)}) %copy-start.2) | copy-done | bytes 131096
  5.8 0.0 copy-start.3
  5.8 0.9 %copy-done.3 = bf16[256,256]{1,0:T(8,128)(2,1)S(1)} copy-done((bf16[256,256]{1,0:T(8,128)(2,1)S(1)}, bf16[256,256]{1,0:T(8,128)(2,1)}, u32[]{:S(2)}) %copy-start.3) | copy-done | bytes 131096
  6.7 0.0 copy-start.4
  6.7 0.9 %copy-done.4 = bf16[1,4,12544]{2,1,0:T(4,128)(2,1)S(1)} copy-done((bf16[1,4,12544]{2,1,0:T(4,128)(2,1)S(1)}, bf16[1,4,12544]{2,1,0:T(4,128)(2,1)}, u32[]{:S(2)}) %copy-start.4) | copy-done | bytes 100376
  7.6 0.0 copy-start.5
  7.6 0.9 %copy-done.5 = bf16[1,4,12544]{2,1,0:T(4,128)(2,1)S(1)} copy-done((bf16[1,4,12544]{2,1,0:T(4,128)(2,1)S(1)}, bf16[1,4,12544]{2,1,0:T(4,128)(2,1)}, u32[]{:S(2)}) %copy-start.5) | copy-done | bytes 100376
  8.5 0.0 copy-start.6
  8.5 0.8 %copy-done.6 = bf16[1,64,512]{2,1,0:T(8,128)(2,1)S(1)} copy-done((bf16[1,64,512]{2,1,0:T(8,128)(2,1)S(1)}, bf16[1,64,512]{2,1,0:T(8,128)(2,1)}, u32[]{:S(2)}) %copy-start.6) | copy-done | bytes 65560
  9.3 49.8 %shard_map.138 = (bf16[4,12544]{1,0:T(4,128)(2,1)S(1)}, f32[256,256]{1,0:T(8,128)S(1)}, f32[256,256]{1,0:T(8,128)S(1)}, f32[512,256]{1,0:T(8,128)S(1)}) custom-call(bf16[4,12544]{1,0:T(4,128)(2,1)S(1)} %bitcast.13, bf16[4,12544]{1,0:T(4,128)(2,1)S(1)} %bitcast.14, bf16[49,49,64]{2,1,0:T(8,128)(2,1)S(1)} %bitcast.12, bf16[64,512]{1,0:T(8,128)(2,1)S(1)} %bitcast.16, ...), custom_call_target="tpu_custom_call" | custom-call | tf_op jit(solution)/shard_map/pallas_call | solution.py:526
  59.2 0.6 %copy.20 = bf16[1,4,12544]{2,1,0:T(4,128)(2,1)} copy(bf16[1,4,12544]{2,1,0:T(4,128)(2,1)S(1)} %bitcast.15) | data formatting | bytes 200704
  59.8 0.7 %copy.21 = f32[256,256]{1,0:T(8,128)} copy(f32[256,256]{1,0:T(8,128)S(1)} %get-tuple-element.17) | data formatting | bytes 524288
  60.5 0.7 %copy.22 = f32[256,256]{1,0:T(8,128)} copy(f32[256,256]{1,0:T(8,128)S(1)} %get-tuple-element.18) | data formatting | bytes 524288
  61.2 0.8 %copy.23 = f32[512,256]{1,0:T(8,128)} copy(f32[512,256]{1,0:T(8,128)S(1)} %get-tuple-element.19) | data formatting | bytes 1048576
  (4 shorter events, 0.0 us)
Async XLA Ops:
  1.3 0.7 %copy-start.8 = (s32[1,64]{1,0:T(1,128)S(1)}, s32[1,64]{1,0:T(1,128)}, u32[]{:S(2)}) copy-start(s32[1,64]{1,0:T(1,128)} %param.16) | copy-start | bytes 772
  1.3 0.7 %copy-start.9 = (s32[1,64,1]{1,2,0:T(1,128)S(1)}, s32[1,64,1]{1,2,0:T(1,128)}, u32[]{:S(2)}) copy-start(s32[1,64,1]{1,2,0:T(1,128)} %param.15) | copy-start | bytes 772
  2.0 0.7 %copy-start.7 = (s32[1,64]{1,0:T(1,128)S(1)}, s32[1,64]{1,0:T(1,128)}, u32[]{:S(2)}) copy-start(s32[1,64]{1,0:T(1,128)} %tgt.1) | copy-start | bytes 772
  2.9 1.1 %copy-start = (bf16[1,49,49,64]{3,2,1,0:T(8,128)(2,1)S(1)}, bf16[1,49,49,64]{3,2,1,0:T(8,128)(2,1)}, u32[]{:S(2)}) copy-start(bf16[1,49,49,64]{3,2,1,0:T(8,128)(2,1)} %param.13) | copy-start | bytes 921988
  4.0 0.9 %copy-start.1 = (bf16[512,256]{1,0:T(8,128)(2,1)S(1)}, bf16[512,256]{1,0:T(8,128)(2,1)}, u32[]{:S(2)}) copy-start(bf16[512,256]{1,0:T(8,128)(2,1)} %w_rad.1) | copy-start | bytes 786436
  4.9 0.9 %copy-start.2 = (bf16[256,256]{1,0:T(8,128)(2,1)S(1)}, bf16[256,256]{1,0:T(8,128)(2,1)}, u32[]{:S(2)}) copy-start(bf16[256,256]{1,0:T(8,128)(2,1)} %w_src.1) | copy-start | bytes 393220
  5.8 0.9 %copy-start.3 = (bf16[256,256]{1,0:T(8,128)(2,1)S(1)}, bf16[256,256]{1,0:T(8,128)(2,1)}, u32[]{:S(2)}) copy-start(bf16[256,256]{1,0:T(8,128)(2,1)} %w_tgt.1) | copy-start | bytes 393220
  6.7 0.9 %copy-start.4 = (bf16[1,4,12544]{2,1,0:T(4,128)(2,1)S(1)}, bf16[1,4,12544]{2,1,0:T(4,128)(2,1)}, u32[]{:S(2)}) copy-start(bf16[1,4,12544]{2,1,0:T(4,128)(2,1)} %param.11) | copy-start | bytes 301060
  7.6 0.9 %copy-start.5 = (bf16[1,4,12544]{2,1,0:T(4,128)(2,1)S(1)}, bf16[1,4,12544]{2,1,0:T(4,128)(2,1)}, u32[]{:S(2)}) copy-start(bf16[1,4,12544]{2,1,0:T(4,128)(2,1)} %param.12) | copy-start | bytes 301060
  8.5 0.8 %copy-start.6 = (bf16[1,64,512]{2,1,0:T(8,128)(2,1)S(1)}, bf16[1,64,512]{2,1,0:T(8,128)(2,1)}, u32[]{:S(2)}) copy-start(bf16[1,64,512]{2,1,0:T(8,128)(2,1)} %param.14) | copy-start | bytes 196612

commit v2 on v1

--- a/solution.py
+++ b/solution.py
@@ -188,21 +188,34 @@
 def block_kernel(
     peers,
     scale,
+    emb_hbm,
+    cot_hbm,
+    rot_hbm,
+    dist_hbm,
+    owner_hbm,
+    local_hbm,
+    tgt_hbm,
+    live_hbm,
+    w_src_hbm,
+    w_tgt_hbm,
+    w_rad_hbm,
+    out_embed,
+    out_src,
+    out_tgt,
+    out_rad,
     emb,
     cot,
     rot,
     dist,
-    keys,
+    owner,
+    local,
+    near_tgt,
     tgt,
     live,
     w_src,
     w_tgt,
     w_rad,
-    out_embed,
-    out_src,
-    out_tgt,
-    out_rad,
-    atoms,
+    x_all,
     y_all,
     y_tgt,
     rot_rows,
@@ -218,17 +231,14 @@
     from_x,
     to_z,
     from_z,
-    part_tgt,
-    part_rad,
-    part_src,
-    core_tgt,
-    core_rad,
-    core_src,
-    early,
-    early_in,
-    late,
-    late_in,
+    share,
+    core_in,
+    both,
+    both_x,
+    both_z,
+    both_in,
     whole,
+    load,
     y_send,
     y_recv,
     f_send,
@@ -238,10 +248,10 @@
     z_recv,
     c_send,
     c_recv,
+    d_send,
+    d_recv,
     e_send,
     e_recv,
-    l_send,
-    l_recv,
     g_send,
     g_recv,
     h_send,
@@ -259,6 +269,24 @@
     beside = {"graph": z * 2 + 1 - x}
     other = {"dp": 1 - core}
     started = []
+    loads = {}
+    pairs = (
+        ("emb", emb_hbm, emb),
+        ("w_rad", w_rad_hbm, w_rad),
+        ("dist", dist_hbm, dist),
+        ("live", live_hbm, live),
+        ("tgt", tgt_hbm, tgt),
+        ("rot", rot_hbm, rot),
+        ("cot", cot_hbm, cot),
+        ("owner", owner_hbm, owner),
+        ("local", local_hbm, local),
+        ("near_tgt", tgt_hbm, near_tgt),
+        ("w_src", w_src_hbm, w_src),
+        ("w_tgt", w_tgt_hbm, w_tgt),
+    )
+    for index, (name, far, near) in enumerate(pairs):
+        loads[name] = pltpu.make_async_copy(far, near, load.at[index])
+        loads[name].start()
 
     def send(*args):
         copy = remote(*args)
@@ -272,15 +300,13 @@
         remote(ref, ref, sem, sem, other).wait_recv()
 
     barrier = pltpu.get_barrier_semaphore()
-    for step in range(1, peers):
+    line = [{"graph": lax.rem(z + step, columns) * 2 + x} for step in range(1, columns)]
+    for device in line + [beside, other]:
         pl.semaphore_signal(
-            barrier,
-            inc=1,
-            device_id={"graph": lax.rem(me + step, peers)},
-            device_id_type=pl.DeviceIdType.MESH,
-        )
-    pl.semaphore_signal(barrier, inc=1, device_id=other, device_id_type=pl.DeviceIdType.MESH)
-
+            barrier, inc=1, device_id=device, device_id_type=pl.DeviceIdType.MESH
+        )
+
+    loads["emb"].wait()
     for group in range(groups):
         rows = []
         for c in range(4 * group, 4 * group + 4):
@@ -288,15 +314,16 @@
                 rows.append(emb[:, c * width : (c + 1) * width].astype(jnp.float32))
             else:
                 rows.append(jnp.zeros((atom_count, width), jnp.float32))
-        atoms[16 * group : 16 * group + 16, :] = jnp.concatenate(rows, axis=0).astype(jnp.bfloat16)
-    y_all[me] = dot(atoms[...], w_src[...]).astype(jnp.bfloat16)
-    pl.semaphore_wait(barrier, peers)
+        x_all[me, 16 * group : 16 * group + 16, :] = jnp.concatenate(rows, axis=0).astype(jnp.bfloat16)
+    own = x_all.at[me]
+    pl.semaphore_wait(barrier, columns + 1)
     for step in range(1, columns):
         to = {"graph": lax.rem(z + step, columns) * 2 + x}
-        send(y_all.at[me], y_all.at[me], y_send.at[step], y_recv.at[me], to)
-    send(y_all.at[me], y_all.at[me], y_send.at[0], y_recv.at[me], beside)
-    y_tgt[...] = dot(atoms[...], w_tgt[...]).astype(jnp.bfloat16)
-
+        send(own, own, y_send.at[step], y_recv.at[me], to)
+    send(own, own, y_send.at[0], y_recv.at[me], beside)
+
+    for name in ("w_rad", "dist", "live", "tgt", "rot", "cot", "owner", "local", "near_tgt"):
+        loads[name].wait()
     pre = dot(dist[...], w_rad[...])
     sig = jax.nn.sigmoid(pre)
     alive = lax.broadcasted_iota(jnp.int32, (edges, width), 0) < live[0, 0]
@@ -306,8 +333,10 @@
     row = lax.broadcasted_iota(jnp.int32, (256, 256), 0)
     k, a = lax.rem(lax.div(row, 4), 4), lax.rem(row, 4)
     src_rows = 16 * peers
-    key_src = jnp.broadcast_to(keys[0:1, :], (256, 256))
-    key_tgt = jnp.broadcast_to(keys[1:2, :], (256, 256))
+    fold = lax.div(lax.broadcasted_iota(jnp.int32, (256, 256), 1), edges)
+    named = owner[...] * 4 + local[...]
+    key_src = jnp.concatenate([named] * 4, axis=1) + fold * (4 * peers)
+    key_tgt = jnp.concatenate([near_tgt[...]] * 4, axis=1) + fold * 4
     hit_src = (k * (4 * peers) + lax.div(row, 16) * 4 + a) == key_src
     hit_tgt = (k * 4 + a) == key_tgt
     hit = ((row < src_rows) & hit_src) | ((row >= src_rows) & (row < src_rows + 16) & hit_tgt)
@@ -336,8 +365,8 @@
 
     def forward(step):
         block = lax.rem(z - step + columns, columns) * 2 + x
-        arrived(y_all.at[block], y_recv.at[block])
-        send(y_all.at[block], y_all.at[block], f_send.at[step], y_recv.at[block], beside)
+        arrived(x_all.at[block], y_recv.at[block])
+        send(x_all.at[block], x_all.at[block], f_send.at[step], y_recv.at[block], beside)
 
     for part in range(4):
         lax.fori_loop(part * (edges // 4), (part + 1) * (edges // 4), edge, 0, unroll=8)
@@ -355,19 +384,28 @@
                 jnp.bfloat16
             )
         kept[16 * group : 16 * group + 16, :] = total[src_rows : src_rows + 16].astype(jnp.bfloat16)
-    for step in list(range(1, columns)) + [0]:
+    def across(step):
         goal = lax.rem(z + step, columns)
         send(sums.at[goal * 2 + 1 - x], from_x.at[goal], x_send.at[step], x_recv.at[goal], beside)
 
+    early = max(1, columns - 2)
+    for step in range(1, early + 1):
+        across(step)
+
     half = width // 2
-    part_tgt[...] = (
-        dot(atoms[...], kept[...], FIRST).astype(jnp.bfloat16).reshape(part_tgt.shape)
-    )
-    send(part_tgt.at[1 - core], core_tgt, c_send.at[0], c_recv.at[0], other)
+    cut, wider = half // peers, w_rad.shape[0] // 2 // peers
+    split = cut + wider
+    loads["w_src"].wait()
+    loads["w_tgt"].wait()
+    grad = dot(x_all[me], kept[...], FIRST).astype(jnp.bfloat16)
+    share[:, :, 0:cut, :] = grad.reshape(2, peers, cut, width)
+    y_tgt[...] = dot(x_all[me], w_tgt[...]).astype(jnp.bfloat16)
 
     for step in range(columns):
         block = step * 2 + 1 - x
-        arrived(y_all.at[block], y_recv.at[block])
+        arrived(x_all.at[block], y_recv.at[block])
+    for p in range(peers):
+        y_all[p] = dot(x_all[p], w_src[...]).astype(jnp.bfloat16)
     gate_grad = jnp.zeros((edges, width), jnp.float32)
     spare = jnp.zeros((256 - src_rows - 16, width), jnp.bfloat16)
     for group in range(groups):
@@ -378,10 +416,24 @@
         )
         gate_grad = gate_grad + jnp.sum(mixed.reshape(4, edges, width), axis=0)
     pre_grad = (gate_grad * slope[...]).astype(jnp.bfloat16)
-    part_rad[...] = dot(dist[...], pre_grad, FIRST).astype(jnp.bfloat16).reshape(part_rad.shape)
-    send(part_rad.at[1 - core], core_rad, c_send.at[1], c_recv.at[1], other)
-
-    for step in range(1, columns):
+    grad = dot(dist[...], pre_grad, FIRST).astype(jnp.bfloat16)
+    share[:, :, cut:split, :] = grad.reshape(2, peers, wider, width)
+    tallest = peers * x_all.shape[1]
+    grad = dot(x_all[...].reshape(tallest, width), sums[...].reshape(tallest, width), FIRST)
+    share[:, :, split:, :] = grad.astype(jnp.bfloat16).reshape(2, peers, cut, width)
+    send(share.at[1 - core], core_in, c_send.at[0], c_recv.at[0], other)
+
+    arrived(core_in, c_recv.at[0])
+    both[...] = (share[core].astype(jnp.float32) + core_in[...].astype(jnp.float32)).astype(
+        jnp.bfloat16
+    )
+    for step in list(range(1, columns)) + [0]:
+        goal = lax.rem(z + step, columns)
+        send(both.at[goal * 2 + 1 - x], both_x.at[goal], d_send.at[step], d_recv.at[goal], beside)
+    for step in list(range(early + 1, columns)) + [0]:
+        across(step)
+
+    def along(step):
         goal = lax.rem(z + step, columns)
         arrived(from_x.at[goal], x_recv.at[goal])
         to_z[goal] = (
@@ -389,16 +441,33 @@
         ).astype(jnp.bfloat16)
         send(to_z.at[goal], from_z.at[z], z_send.at[step], z_recv.at[z], {"graph": goal * 2 + x})
 
-    arrived(core_tgt, c_recv.at[0])
-    arrived(core_rad, c_recv.at[1])
-    cut_tgt, cut_rad = half // peers, w_rad.shape[0] // 2 // peers
-    both_tgt = part_tgt[core].astype(jnp.float32) + core_tgt[...].astype(jnp.float32)
-    both_rad = part_rad[core].astype(jnp.float32) + core_rad[...].astype(jnp.float32)
-    early[:, 0:cut_tgt, :] = both_tgt.reshape(peers, cut_tgt, width).astype(jnp.bfloat16)
-    early[:, cut_tgt:, :] = both_rad.reshape(peers, cut_rad, width).astype(jnp.bfloat16)
-    for step in range(1, peers):
-        p = lax.rem(me + step, peers)
-        send(early.at[p], early_in.at[me], e_send.at[step], e_recv.at[me], {"graph": p})
+    for step in range(1, early + 1):
+        along(step)
+
+    for step in range(1, columns):
+        goal = lax.rem(z + step, columns)
+        arrived(both_x.at[goal], d_recv.at[goal])
+        both_z[goal] = (
+            both[goal * 2 + x].astype(jnp.float32) + both_x[goal].astype(jnp.float32)
+        ).astype(jnp.bfloat16)
+        to = {"graph": goal * 2 + x}
+        send(both_z.at[goal], both_in.at[z], e_send.at[step], e_recv.at[z], to)
+    arrived(both_x.at[z], d_recv.at[z])
+    first = both[me].astype(jnp.float32) + both_x[z].astype(jnp.float32)
+    for step in range(1, columns):
+        origin = lax.rem(z + step, columns)
+        arrived(both_in.at[origin], e_recv.at[origin])
+        first = first + both_in[origin].astype(jnp.float32)
+    whole[core, me] = first.astype(jnp.bfloat16)
+    mine = whole.at[core, me]
+    for step in range(1, columns):
+        to = {"graph": lax.rem(z + step, columns) * 2 + x}
+        send(mine, mine, g_send.at[step], g_recv.at[me], to)
+    send(mine, mine, g_send.at[0], g_recv.at[me], beside)
+    send(mine, mine, h_send.at[0], h_recv.at[me], other)
+
+    for step in range(early + 1, columns):
+        along(step)
 
     arrived(from_x.at[z], x_recv.at[z])
     total = sums[me].astype(jnp.float32) + from_x[z].astype(jnp.float32)
@@ -407,53 +476,33 @@
         arrived(from_z.at[origin], z_recv.at[origin])
         total = total + from_z[origin].astype(jnp.float32)
     total = total.astype(jnp.bfloat16)
-    part_src[...] = dot(atoms[...], total, FIRST).astype(jnp.bfloat16).reshape(part_src.shape)
-    send(part_src.at[1 - core], core_src, c_send.at[2], c_recv.at[2], other)
     back = dot(total, w_src[...], LAST) + dot(kept[...], w_tgt[...], LAST)
     for c in range(coeffs):
         out_embed[:, c * width : (c + 1) * width] = back[4 * c : 4 * c + 4].astype(jnp.bfloat16)
-    arrived(core_src, c_recv.at[2])
-    both_src = part_src[core].astype(jnp.float32) + core_src[...].astype(jnp.float32)
-    late[...] = both_src.reshape(late.shape).astype(jnp.bfloat16)
-    for step in range(1, peers):
-        p = lax.rem(me + step, peers)
-        send(late.at[p], late_in.at[me], l_send.at[step], l_recv.at[me], {"graph": p})
-
-    first = early[me].astype(jnp.float32)
-    second = late[me].astype(jnp.float32)
-    for step in range(1, peers):
-        p = lax.rem(me + step, peers)
-        arrived(early_in.at[p], e_recv.at[p])
-        first = first + early_in[p].astype(jnp.float32)
-    for step in range(1, peers):
-        p = lax.rem(me + step, peers)
-        arrived(late_in.at[p], l_recv.at[p])
-        second = second + late_in[p].astype(jnp.float32)
-    split = cut_tgt + cut_rad
-    whole[core, me, 0:split, :] = first.astype(jnp.bfloat16)
-    whole[core, me, split:, :] = second.astype(jnp.bfloat16)
-    mine = whole.at[core, me]
-    for step in range(1, peers):
-        p = lax.rem(me + step, peers)
-        send(mine, mine, g_send.at[step], g_recv.at[me], {"graph": p})
-    send(mine, mine, h_send.at[0], h_recv.at[me], other)
-
     def spread(c, p):
         piece = whole[c, p].astype(jnp.float32) * scale
-        at_tgt = pl.ds(pl.multiple_of(c * half + p * cut_tgt, cut_tgt), cut_tgt)
-        at_rad = pl.ds(pl.multiple_of((c * peers + p) * cut_rad, cut_rad), cut_rad)
-        out_tgt[at_tgt, :] = piece[0:cut_tgt]
-        out_rad[at_rad, :] = piece[cut_tgt:split]
+        at_tgt = pl.ds(pl.multiple_of(c * half + p * cut, cut), cut)
+        at_rad = pl.ds(pl.multiple_of((c * peers + p) * wider, wider), wider)
+        out_tgt[at_tgt, :] = piece[0:cut]
+        out_rad[at_rad, :] = piece[cut:split]
         out_src[at_tgt, :] = piece[split:]
 
     spread(core, me)
-    for step in range(1, peers):
-        p = lax.rem(me + step, peers)
-        arrived(whole.at[core, p], g_recv.at[p])
-        send(whole.at[core, p], whole.at[core, p], h_send.at[step], h_recv.at[p], other)
+    for step in range(1, columns):
+        p = lax.rem(z + columns - step, columns) * 2 + x
+        piece = whole.at[core, p]
+        arrived(piece, g_recv.at[p])
+        send(piece, piece, g_send.at[columns + step], g_recv.at[p], beside)
+        send(piece, piece, h_send.at[step], h_recv.at[p], other)
+        spread(core, p)
+    for step in range(columns):
+        p = lax.rem(z + columns - step, columns) * 2 + 1 - x
+        piece = whole.at[core, p]
+        arrived(piece, g_recv.at[p])
+        send(piece, piece, h_send.at[columns + step], h_recv.at[p], other)
         spread(core, p)
     for step in range(peers):
-        p = lax.rem(me + step, peers)
+        p = lax.rem(me + peers - step, peers)
         arrived(whole.at[1 - core, p], h_recv.at[p])
         spread(1 - core, p)
     for copy in started:
@@ -482,19 +531,28 @@
     tall = -(-groups * 4 // 8) * 8
     deep = -(-tall // 16) * 16
     scale = 1.0 / math.sqrt(lax.axis_size("dp") * edges * peers * coeffs)
-    lane = jnp.arange(4, dtype=jnp.int32)[:, None]
-    key_src = lane * (4 * peers) + (src_owner[0, :, 0] * atom_count + src_local[0])[None, :]
-    key_tgt = lane * 4 + tgt_local[0][None, :]
-    keys = jnp.stack([key_src.reshape(-1), key_tgt.reshape(-1)])
-    half, cut = width // 2, width // 2 // peers
+    cut = width // 2 // peers
     rows = 16 * groups
     bf16, f32 = jnp.bfloat16, jnp.float32
     split = cut + radial // 2 // peers
     vmem = pl.BlockSpec(memory_space=pltpu.VMEM)
-    smem = pl.BlockSpec(memory_space=pltpu.SMEM)
+    hbm = pl.BlockSpec(memory_space=pltpu.HBM)
     dma = pltpu.SemaphoreType.DMA
+    i32 = jnp.int32
     scratch = [
-        pltpu.VMEM((rows, width), bf16),
+        pltpu.VMEM(embed.shape[1:], bf16),
+        pltpu.VMEM(cotangent.shape[1:], bf16),
+        pltpu.VMEM(rotation.shape[1:], bf16),
+        pltpu.VMEM(distance_feat.shape[1:], bf16),
+        pltpu.VMEM((1, edges), i32),
+        pltpu.VMEM((1, edges), i32),
+        pltpu.VMEM((1, edges), i32),
+        pltpu.SMEM((1, edges), i32),
+        pltpu.SMEM((1, 1), i32),
+        pltpu.VMEM(w_src.shape, bf16),
+        pltpu.VMEM(w_tgt.shape, bf16),
+        pltpu.VMEM(w_radial.shape, bf16),
+        pltpu.VMEM((peers, rows, width), bf16),
         pltpu.VMEM((peers, rows, width), bf16),
         pltpu.VMEM((rows, width), bf16),
         pltpu.VMEM((tall * edges, 128), f32),
@@ -510,19 +568,15 @@
         pltpu.VMEM((columns, rows, width), bf16),
         pltpu.VMEM((columns, rows, width), bf16),
         pltpu.VMEM((columns, rows, width), bf16),
-        pltpu.VMEM((2, half, width), bf16),
-        pltpu.VMEM((2, radial // 2, width), bf16),
-        pltpu.VMEM((2, half, width), bf16),
-        pltpu.VMEM((half, width), bf16),
-        pltpu.VMEM((radial // 2, width), bf16),
-        pltpu.VMEM((half, width), bf16),
-        pltpu.VMEM((peers, split, width), bf16),
-        pltpu.VMEM((peers, split, width), bf16),
-        pltpu.VMEM((peers, cut, width), bf16),
-        pltpu.VMEM((peers, cut, width), bf16),
+        pltpu.VMEM((2, peers, split + cut, width), bf16),
+        pltpu.VMEM((peers, split + cut, width), bf16),
+        pltpu.VMEM((peers, split + cut, width), bf16),
+        pltpu.VMEM((columns, split + cut, width), bf16),
+        pltpu.VMEM((columns, split + cut, width), bf16),
+        pltpu.VMEM((columns, split + cut, width), bf16),
         pltpu.VMEM((2, peers, split + cut, width), bf16),
     ]
-    counts = [peers, peers, columns, columns, columns, columns, columns, 3, 3] + [peers] * 8
+    counts = [12, peers, peers] + [columns] * 5 + [1, 1] + [columns] * 4 + [peers] * 4
     grad_embed, grad_src, grad_tgt, grad_rad = pl.pallas_call(
         functools.partial(block_kernel, peers, scale),
         out_shape=(
@@ -531,18 +585,19 @@
             jax.ShapeDtypeStruct((width, width), f32),
             jax.ShapeDtypeStruct((radial, width), f32),
         ),
-        in_specs=[vmem] * 5 + [smem] * 2 + [vmem] * 3,
+        in_specs=[hbm] * 11,
         out_specs=(vmem,) * 4,
         scratch_shapes=scratch + [dma((count,)) for count in counts],
         compiler_params=pltpu.CompilerParams(
-            collective_id=0, has_side_effects=True, vmem_limit_bytes=40 * 1024 * 1024
+            collective_id=0, has_side_effects=True, vmem_limit_bytes=63 * 1024 * 1024
         ),
     )(
         embed[0],
         cotangent[0],
         rotation[0],
         distance_feat[0],
-        keys,
+        src_owner.reshape(1, edges),
+        src_local,
         tgt_local,
         live_count,
         w_src,

time: 62.4 us -> 54 us (0.87)
  local copies, waits for them, and re-layouts: 10.7 us -> 4.84 us
  Pallas kernels: 49.8 us -> 47.7 us
    unnamed x24 -> x8, local copies, waits for them, and re-layouts: 10.6 us -> 4.84 us
    pallas_call x1, Pallas kernels: 49.8 us -> 47.7 us  [near_shards(): pl.pallas_call(functools.partial(block_kernel, peers, scale), out_shape=(...]
where the time goes in v2:
time: 54 us; the launch traced here: 53.8 us
  Pallas kernels  47.7 us (88%)
  local copies, waits for them, and re-layouts  4.84 us (9%)
  between operations  1.3 us (2%)
    pallas_call x1, Pallas kernels, near_shards(): pl.pallas_call(functools.partial(block_kernel, peers, scale), out_shape=(...  47.7 us
    unnamed x8, local copies, waits for them, and re-layouts  4.84 us

profile of v2, /device:TPU:0, one launch (start us, length us, event | category | flops | bytes accessed | tf_op | source)
XLA Modules:
  0.0 53.8 jit_solution(1071672908153478780)
XLA Ops:
  1.3 47.7 %shard_map.138 = (bf16[4,12544]{1,0:T(4,128)(2,1)}, f32[256,256]{1,0:T(8,128)}, f32[256,256]{1,0:T(8,128)}, f32[512,256]{1,0:T(8,128)}) custom-call(bf16[4,12544]{1,0:T(4,128)(2,1)} %bitcast.7, bf16[4,12544]{1,0:T(4,128)(2,1)} %bitcast.8, bf16[49,49,64]{2,1,0:T(8,128)(2,1)} %bitcast.6, bf16[64,512]{1,0:T(8,128)(2,1)} %bitcast.10, s32[1,64]{1,0:T(1,128)} %bitcast.11, ...), custom_call_target="tpu_custom_call" | custom-call | tf_op jit(solution)/shard_map/pallas_call | solution.py:580
  49.0 0.0 copy-start.1
  49.0 1.6 %copy.20 = bf16[1,4,12544]{2,1,0:T(4,128)(2,1)} copy(bf16[1,4,12544]{2,1,0:T(4,128)(2,1)} %bitcast.9) | data formatting | bytes 200704
  50.6 0.0 copy-start
  50.6 1.7 %copy.21 = f32[256,256]{1,0:T(8,128)} copy(f32[256,256]{1,0:T(8,128)} %get-tuple-element.17) | data formatting | bytes 524288
  52.3 0.0 copy-done.1
  52.3 0.7 %copy.22 = f32[256,256]{1,0:T(8,128)} copy(f32[256,256]{1,0:T(8,128)S(1)} %copy-done.1) | data formatting | bytes 524288
  53.0 0.0 copy-done
  53.0 0.8 %copy.23 = f32[512,256]{1,0:T(8,128)} copy(f32[512,256]{1,0:T(8,128)S(1)} %copy-done) | data formatting | bytes 1048576
Async XLA Ops:
  49.0 3.4 %copy-start.1 = (f32[256,256]{1,0:T(8,128)S(1)}, f32[256,256]{1,0:T(8,128)}, u32[]{:S(2)}) copy-start(f32[256,256]{1,0:T(8,128)} %get-tuple-element.18) | copy-start | bytes 786436
  50.6 2.4 %copy-start = (f32[512,256]{1,0:T(8,128)S(1)}, f32[512,256]{1,0:T(8,128)}, u32[]{:S(2)}) copy-start(f32[512,256]{1,0:T(8,128)} %get-tuple-element.19) | copy-start | bytes 1572868
